TPU v7x, 512 devices: a whole 4x8x8 slice. The times are simulated.
512 devices in a mesh: grp: 32 (over x_hi, y, core), tp: 16 (over x_lo, z).
Axes of the slice: x: 4 (x_hi: 2, x_lo: 2; x = x_hi * 2 + x_lo), y: 8, z: 8, core: 2. Of those that a mesh axis runs over, the one named last changes fastest.
Arguments:
- hidden: bfloat16 [2048, 8192], P('grp'), may hold values from -6 to 6
- w_proj: bfloat16 [8192, 5120], P('grp', 'tp'), may hold values from -0.0625 to 0.0625
- cache_keys: bfloat16 [32, 2048, 512], P('grp', 'tp')
- cache_values: bfloat16 [32, 2048, 512], P('grp', 'tp'), may hold values from -24 to 24
- cand_issue: int32 [1024], P('grp'), may hold values from 0 to 31, as said below
- cand_length: int32 [1024], P('grp'), may hold values from 0 to 4, as said below
- prefix_len: int32 [32], P('grp'), may hold values from 256 to 2048, as said below
Outputs:
- attended: bfloat16 [2048, 4096], P('grp', 'tp')
Inputs may be any that keep to these rules, and one draw needn't show every extreme that they name: `cand_length`: each anchor's 32 entries hold its candidates in order, then zeros; the lengths of one anchor sum to 64; every candidate but the last has 2 tokens or more, and the first has exactly 4. `cand_issue`: the candidates of one anchor name different issues; entries with length 0 are unused; issue i belongs to index i of grp. `prefix_len`: some issue has exactly 2048 cached positions.
All inputs are finite; a program needn't handle non-finite values.
Results may differ from a plain program's by a relative error of at most 0.012.
Values may be sent and summed in bfloat16 or wider, within the bound.
A program may use at most 64 MiB of HBM per device.

v0:
```python
import math

import jax
import jax.numpy as jnp
from jax import lax
from jax.sharding import PartitionSpec as P

HEADS = 32
HD = 128


NEGATIVE = -1e30
THETA = 1000000.0


def row_layout(cand_issue, cand_length, rows):
    ends = jnp.cumsum(cand_length)
    starts = ends - cand_length
    index = jnp.arange(rows)
    member = ((starts[None, :] <= index[:, None]) & (index[:, None] < ends[None, :])).astype(
        jnp.int32
    )
    issue = jnp.sum(member * cand_issue[None, :], axis=1)
    position = index - jnp.sum(member * starts[None, :], axis=1)
    return (issue, position)


def rotary(values, positions):
    width = values.shape[-1]
    half = width // 2
    freq = THETA ** (-2.0 * jnp.arange(half).astype(jnp.float32) / width)
    angle = positions.astype(jnp.float32)[:, None] * freq[None, :]
    cosine = jnp.cos(angle)[:, None, :]
    sine = jnp.sin(angle)[:, None, :]
    first = values[..., :half]
    second = values[..., half:]
    return jnp.concatenate(
        [first * cosine - second * sine, second * cosine + first * sine], axis=-1
    )


def local(hidden, w_proj, cache_keys, cache_values, cand_issue, cand_length, prefix_len):
    rows = hidden.shape[0]
    groups = lax.axis_size("grp")
    ranks = lax.axis_size("tp")
    cols = w_proj.shape[1]
    block = cache_keys.shape[1]
    kv_width = cache_keys.shape[2]
    head_dim = HD
    heads = HEADS
    kv_heads = kv_width // head_dim
    group = heads // kv_heads
    per_rank = heads // ranks
    q_cols = heads * head_dim // ranks
    k_cols = kv_width // ranks
    cap = 2 * ((rows + groups - 1) // groups)
    slots = groups * cap
    scale = 1.0 / math.sqrt(head_dim)
    tp_index = lax.axis_index("tp")
    projected = jnp.dot(
        hidden,
        lax.all_gather(w_proj, "grp", axis=0, tiled=True),
        preferred_element_type=jnp.float32,
    )
    projected = projected.astype(jnp.bfloat16)
    issue, position = row_layout(cand_issue, cand_length, rows)
    target = issue * cap + position
    slot_index = jnp.arange(slots)
    table = (slot_index[:, None] == target[None, :]).astype(jnp.bfloat16)
    packed = (
        jnp.dot(table, projected, preferred_element_type=jnp.float32)
        .astype(jnp.bfloat16)
        .reshape(groups, cap, cols)
    )
    counts = jnp.sum((jnp.arange(groups)[:, None] == issue[None, :]).astype(jnp.float32), axis=1)
    counts = counts.reshape(groups, 1).astype(jnp.bfloat16)
    received, sizes = (
        lax.all_to_all(packed, "grp", split_axis=0, concat_axis=0, tiled=True),
        lax.all_to_all(counts, "grp", split_axis=0, concat_axis=0, tiled=True),
    )
    everything = lax.all_gather(received, "tp", axis=2, tiled=True).reshape(slots, ranks, cols)
    queries = everything[:, :, :q_cols].reshape(slots, heads, head_dim)
    keys_new = everything[:, :, q_cols : q_cols + k_cols].reshape(slots, kv_heads, head_dim)
    values_new = everything[:, :, q_cols + k_cols :].reshape(slots, kv_width)
    slot_anchor = slot_index // cap
    slot_within = slot_index % cap
    prefix = prefix_len[0]
    positions = prefix + slot_within
    q_rot = rotary(queries.astype(jnp.float32), positions).astype(jnp.bfloat16)
    k_rot = rotary(keys_new.astype(jnp.float32), positions).astype(jnp.bfloat16)
    limit = sizes[:, 0].astype(jnp.int32)[slot_anchor]
    own_full = (slot_anchor[:, None] == slot_anchor[None, :]) & (
        slot_within[None, :] <= slot_within[:, None]
    )
    own_full = own_full & (slot_within[None, :] < limit[None, :])
    mask_own = own_full & (tp_index == 0)
    mask_own = jnp.repeat(mask_own, group, axis=0)
    early = (tp_index * block + jnp.arange(block) < prefix)[None, :]
    maxima_list = []
    totals_list = []
    sums_list = []
    for head in range(kv_heads):
        query = q_rot[:, head * group : (head + 1) * group, :].reshape(slots * group, head_dim)
        cached_k = cache_keys[0, :, head * head_dim : (head + 1) * head_dim]
        cached_v = cache_values[0, :, head * head_dim : (head + 1) * head_dim]
        score_p = lax.dot_general(
            query, cached_k, (((1,), (1,)), ((), ())), preferred_element_type=jnp.float32
        )
        score_p = jnp.where(early, score_p * scale, NEGATIVE)
        score_o = lax.dot_general(
            query, k_rot[:, head, :], (((1,), (1,)), ((), ())), preferred_element_type=jnp.float32
        )
        score_o = jnp.where(mask_own, score_o * scale, NEGATIVE)
        top = jnp.maximum(jnp.max(score_p, axis=1), jnp.max(score_o, axis=1))
        w_p = jnp.where(early, jnp.exp(score_p - top[:, None]), 0.0)
        w_o = jnp.where(mask_own, jnp.exp(score_o - top[:, None]), 0.0)
        total = jnp.sum(w_p, axis=1) + jnp.sum(w_o, axis=1)
        mixed = jnp.dot(w_p.astype(jnp.bfloat16), cached_v, preferred_element_type=jnp.float32)
        mixed = mixed + jnp.dot(
            w_o.astype(jnp.bfloat16),
            values_new[:, head * head_dim : (head + 1) * head_dim],
            preferred_element_type=jnp.float32,
        )
        maxima_list.append(top.reshape(slots, group))
        totals_list.append(total.reshape(slots, group))
        sums_list.append(mixed.reshape(slots, group * head_dim))
    maxima = jnp.concatenate(maxima_list, axis=1)
    totals = jnp.concatenate(totals_list, axis=1)
    sums = jnp.concatenate(sums_list, axis=1)
    parts_top, parts_total, parts_mixed = (
        lax.all_to_all(
            maxima.reshape(slots, ranks, per_rank), "tp", split_axis=1, concat_axis=0, tiled=True
        ),
        lax.all_to_all(
            totals.reshape(slots, ranks, per_rank), "tp", split_axis=1, concat_axis=0, tiled=True
        ),
        lax.all_to_all(
            sums.reshape(slots, ranks, per_rank * head_dim),
            "tp",
            split_axis=1,
            concat_axis=0,
            tiled=True,
        ),
    )
    parts_top = parts_top.reshape(ranks, slots, per_rank)
    parts_total = parts_total.reshape(ranks, slots, per_rank)
    parts_mixed = parts_mixed.reshape(ranks, slots, per_rank, head_dim)
    top = jnp.max(parts_top, axis=0)
    factor = jnp.exp(parts_top - top[None])
    total = jnp.sum(parts_total * factor, axis=0)
    mixed = jnp.sum(parts_mixed * factor[..., None], axis=0)
    result = mixed / total[..., None]
    attended_slots = result.reshape(groups, cap, per_rank * head_dim).astype(jnp.bfloat16)
    returned = lax.all_to_all(attended_slots, "grp", split_axis=0, concat_axis=0, tiled=True)
    back = (target[:, None] == slot_index[None, :]).astype(jnp.bfloat16)
    return jnp.dot(
        back, returned.reshape(slots, per_rank * head_dim), preferred_element_type=jnp.float32
    ).astype(jnp.bfloat16)


def solution(mesh):
    placed = (
        P("grp", None),
        P("grp", "tp"),
        P("grp", "tp", None),
        P("grp", "tp", None),
        P("grp"),
        P("grp"),
        P("grp"),
    )
    return jax.shard_map(
        local, mesh=mesh, in_specs=placed, out_specs=P("grp", "tp"), check_vma=False
    )
```

profile of v0, /device:TPU:1, one launch (start us, length us, event | category | flops | bytes accessed | tf_op | source)
XLA Modules:
  0.0 369.1 jit_solution(12952678807569898592)
XLA Ops:
  9.6 104.3 %all-gather.3.cloned.1.call-done = bf16[8192,320]{0,1:T(8,128)(2,1)} async-done(((bf16[256,320]{0,1:T(8,128)(2,1)}), bf16[8192,320]{0,1:T(8,128)(2,1)}) %all-gather.3.cloned.1.call-update) | async-done | bytes 5242896 | tf_op jit(solution)/shard_map/all_gather | solution.py:62
  113.9 4.3 %convolution_convert_fusion = bf16[128,320]{0,1:T(8,128)(2,1)S(1)} fusion(bf16[64,8192]{1,0:T(8,128)(2,1)S(1)} %copy-done, bf16[8192,320]{0,1:T(8,128)(2,1)} %all-gather.3.cloned.1.call-done, s32[64]{0:T(128)S(1)} %subtract_add_fusion), kind=kOutput, calls=%fused_computation.26 | convolution fusion | flops 340856832 | bytes 6373632 | tf_op jit(solution)/shard_map/dot_general | solution.py:71
  118.5 14.2 %all_to_all.61 = bf16[32,4,320]{2,1,0:T(4,128)(2,1)S(1)} all-to-all(bf16[32,4,320]{2,1,0:T(4,128)(2,1)S(1)} %reshape.358), channel_id=1, replica_groups=mesh['grp'=32,'tp'=16] {'grp'}, dimensions={0} | all-to-all | bytes 163840 | tf_op jit(solution)/shard_map/all_to_all | solution.py:78
  134.5 5.0 %all-to-all-start.1 = ((bf16[32,1,1]{2,1,0:T(2,128)(2,1)}), bf16[32,1,1]{2,1,0:T(2,128)(2,1)S(1)}, u32[]{:S(2)}, u32[]{:S(2)}) async-start(bf16[32,1,1]{2,1,0:T(2,128)(2,1)} %copy.181), calls=%async_computation.1 | async-start | bytes 32768 | tf_op jit(solution)/shard_map/all_to_all | solution.py:79
  141.3 7.6 %all-to-all-done.1 = bf16[32,1,1]{2,1,0:T(2,128)(2,1)S(1)} async-done(((bf16[32,1,1]{2,1,0:T(2,128)(2,1)}), bf16[32,1,1]{2,1,0:T(2,128)(2,1)S(1)}, u32[]{:S(2)}, u32[]{:S(2)}) %all-to-all-start.1) | async-done | bytes 96 | tf_op jit(solution)/shard_map/all_to_all | solution.py:79
  149.6 1.2 gather_fusion
  151.2 53.0 %all-gather.5.cloned.1.call-done = bf16[32,4,5120]{0,1,2:T(4,128)(2,1)} async-done(((bf16[32,4,320]{0,1,2:T(4,128)(2,1)}), bf16[32,4,5120]{0,1,2:T(4,128)(2,1)}) %all-gather.5.cloned.1.call-update) | async-done | bytes 1310736 | tf_op jit(solution)/shard_map/all_gather | solution.py:81
  204.2 8.7 %copy.178 = bf16[32,4,5120]{2,1,0:T(4,128)(2,1)} copy(bf16[32,4,5120]{0,1,2:T(4,128)(2,1)} %all-gather.5.cloned.1.call-done) | data formatting | bytes 2621440 | tf_op jit(solution)/shard_map/all_gather | solution.py:81
  212.9 2.9 reshape.359
  215.9 1.0 fusion.122
  216.9 1.6 slice_convert_fusion
  219.1 1.8 reshape.369
  222.9 1.1 fusion.124
  225.5 1.7 fusion.123
  227.2 1.7 fusion.129
  229.0 1.7 fusion.127
  230.7 2.1 copy.186
  233.8 1.0 max.52
  234.8 1.9 fusion.29
  236.7 2.2 fusion.35
  239.5 1.0 max.53
  240.6 2.2 fusion.33
  243.4 1.0 max.54
  244.5 1.5 fusion.31
  246.0 2.2 convolution_add_fusion
  248.2 1.1 convolution_add_fusion.3
  249.3 1.4 fusion.17
  250.7 1.1 convolution_add_fusion.2
  251.8 1.1 convolution_add_fusion.1
  254.7 1.0 copy.202
  255.7 3.6 all-to-all-start.4
  259.3 1.5 pad_maximum_fusion.1
  260.8 1.0 concatenate.33
  261.8 2.0 copy.199
  263.8 1.0 concatenate.30
  264.8 1.9 copy.196
  266.8 1.3 concatenate.32
  270.1 1.0 copy.200
  271.1 7.6 %all-to-all-start.3 = ((f32[128,16,2]{0,2,1:T(2,128)}), f32[128,16,2]{0,2,1:T(2,128)S(1)}, u32[]{:S(2)}, u32[]{:S(2)}) async-start(f32[128,16,2]{0,2,1:T(2,128)} %copy.200), calls=%async_computation.3 | async-start | bytes 32768 | tf_op jit(solution)/shard_map/all_to_all | solution.py:131
  278.7 2.8 pad_maximum_fusion
  281.6 4.5 %all-to-all-done.3 = f32[128,16,2]{0,2,1:T(2,128)S(1)} async-done(((f32[128,16,2]{0,2,1:T(2,128)}), f32[128,16,2]{0,2,1:T(2,128)S(1)}, u32[]{:S(2)}, u32[]{:S(2)}) %all-to-all-start.3) | async-done | bytes 16416 | tf_op jit(solution)/shard_map/all_to_all | solution.py:131
  286.0 3.9 %all-to-all-start.2 = ((f32[128,16,256]{2,0,1:T(8,128)}), f32[128,16,256]{2,0,1:T(8,128)S(1)}, u32[]{:S(2)}, u32[]{:S(2)}) async-start(f32[128,16,256]{2,0,1:T(8,128)} %pad_maximum_fusion), calls=%async_computation.2 | async-start | bytes 4194304 | tf_op jit(solution)/shard_map/all_to_all | solution.py:137
  290.5 1.4 copy.201
  291.9 4.8 %mul.184 = f32[16,128,2,128]{3,2,1,0:T(2,128)} broadcast(f32[16,128,2]{2,1,0:T(8,128)} %copy.201), dimensions={0,1,2} | broadcast | bytes 2113536 | tf_op jit(solution)/shard_map/mul | solution.py:151
  296.6 3.9 %mul.185 = f32[16,128,1,256]{3,1,0,2:T(8,128)} reshape(f32[16,128,2,128]{3,2,1,0:T(2,128)} %mul.184) | data formatting | bytes 4194304 | tf_op jit(solution)/shard_map/mul | solution.py:151
  300.5 28.5 %all-to-all-done.2 = f32[128,16,256]{2,0,1:T(8,128)S(1)} async-done(((f32[128,16,256]{2,0,1:T(8,128)}), f32[128,16,256]{2,0,1:T(8,128)S(1)}, u32[]{:S(2)}, u32[]{:S(2)}) %all-to-all-start.2) | async-done | bytes 2097184 | tf_op jit(solution)/shard_map/all_to_all | solution.py:137
  329.0 1.9 fusion
  331.0 30.5 %all_to_all.62 = bf16[32,4,256]{2,1,0:T(4,128)(2,1)S(1)} all-to-all(bf16[32,4,256]{2,1,0:T(4,128)(2,1)S(1)} %divide_convert_fusion), channel_id=1, replica_groups=mesh['grp'=32,'tp'=16] {'grp'}, dimensions={0} | all-to-all | bytes 131072 | tf_op jit(solution)/shard_map/all_to_all | solution.py:154
  (113 shorter events, 18.5 us)
Async XLA Ops:
  6.5 107.4 %copy-start = (bf16[64,8192]{1,0:T(8,128)(2,1)S(1)}, bf16[64,8192]{1,0:T(8,128)(2,1)}, u32[]{:S(2)}) copy-start(bf16[64,8192]{1,0:T(8,128)(2,1)} %param.7) | copy-start | bytes 3145732
  6.5 107.4 %all-gather.3.cloned.1.call-start = ((), (), s32[]{:S(2)}) async-start(), calls=%async_computation.6 | async-start | bytes 5406720 | tf_op jit(solution)/shard_map/all_gather | solution.py:62
  7.3 196.9 %all-gather.5.cloned.1.call-start = ((), (), s32[]{:S(2)}) async-start(), calls=%async_computation.7 | async-start | bytes 5570560 | tf_op jit(solution)/shard_map/all_gather | solution.py:81
  9.6 108.6 %copy-start.22 = (s32[64]{0:T(128)}, s32[64]{0:T(128)S(1)}, u32[]{:S(2)}) copy-start(s32[64]{0:T(128)S(1)} %subtract_add_fusion) | copy-start | bytes 772
  134.5 14.4 %all-to-all-start.1 = ((bf16[32,1,1]{2,1,0:T(2,128)(2,1)}), bf16[32,1,1]{2,1,0:T(2,128)(2,1)S(1)}, u32[]{:S(2)}, u32[]{:S(2)}) async-start(bf16[32,1,1]{2,1,0:T(2,128)(2,1)} %copy.181), calls=%async_computation.1 | async-start | bytes 32768 | tf_op jit(solution)/shard_map/all_to_all | solution.py:79
  140.6 100.0 %copy-start.14 = (pred[128]{0:T(512)(128)(4,1)}, pred[128]{0:T(512)(128)(4,1)S(1)}, u32[]{:S(2)}) copy-start(pred[128]{0:T(512)(128)(4,1)S(1)} %add_compare_fusion) | copy-start | bytes 388
  219.1 1.9 copy-start.12
  224.0 1.2 copy-start.13
  244.5 3.7 %copy-start.1 = (f32[1024,128]{0,1:T(8,128)S(1)}, f32[1024,128]{0,1:T(8,128)}, u32[]{:S(2)}) copy-start(f32[1024,128]{0,1:T(8,128)} %get-tuple-element.28) | copy-start | bytes 1572868
  244.5 3.7 %copy-start.9 = (f32[1024,128]{1,0:T(8,128)S(1)}, f32[1024,128]{1,0:T(8,128)}, u32[]{:S(2)}) copy-start(f32[1024,128]{1,0:T(8,128)} %fusion.35) | copy-start | bytes 1572868
  244.5 3.7 %copy-start.11 = (bf16[128,16,32]{0,2,1:T(8,128)(2,1)S(1)}, bf16[128,16,32]{0,2,1:T(8,128)(2,1)}, u32[]{:S(2)}) copy-start(bf16[128,16,32]{0,2,1:T(8,128)(2,1)} %copy.186) | copy-start | bytes 393220
  244.5 4.8 %copy-start.2 = (f32[1024,128]{0,1:T(8,128)S(1)}, f32[1024,128]{0,1:T(8,128)}, u32[]{:S(2)}) copy-start(f32[1024,128]{0,1:T(8,128)} %get-tuple-element.26) | copy-start | bytes 1572868
  244.5 4.8 %copy-start.3 = (f32[1024,128]{0,1:T(8,128)S(1)}, f32[1024,128]{0,1:T(8,128)}, u32[]{:S(2)}) copy-start(f32[1024,128]{0,1:T(8,128)} %get-tuple-element.38) | copy-start | bytes 1572868
  244.5 4.8 %copy-start.4 = (f32[1024,128]{0,1:T(8,128)S(1)}, f32[1024,128]{0,1:T(8,128)}, u32[]{:S(2)}) copy-start(f32[1024,128]{0,1:T(8,128)} %get-tuple-element.34) | copy-start | bytes 1572868
  244.5 4.8 %copy-start.15 = (pred[128]{0:T(512)(128)(4,1)S(1)}, pred[128]{0:T(512)(128)(4,1)}, u32[]{:S(2)}) copy-start(pred[128]{0:T(512)(128)(4,1)} %copy-done.14) | copy-start | bytes 388
  249.3 1.4 copy-start.8
  250.7 2.6 copy-start.20
  250.7 2.6 copy-start.21
  250.7 3.0 copy-start.18
  250.7 3.0 copy-start.19
  250.7 3.3 copy-start.16
  250.7 3.3 copy-start.17
  254.7 6.1 %copy-start.6 = (f32[1024,128]{1,0:T(8,128)S(1)}, f32[1024,128]{1,0:T(8,128)}, u32[]{:S(2)}) copy-start(f32[1024,128]{1,0:T(8,128)} %convolution_add_fusion) | copy-start | bytes 1572868
  255.7 15.4 %all-to-all-start.4 = ((f32[128,16,2]{0,2,1:T(2,128)}), f32[128,16,2]{0,2,1:T(2,128)S(1)}, u32[]{:S(2)}, u32[]{:S(2)}) async-start(f32[128,16,2]{0,2,1:T(2,128)} %copy.202), calls=%async_computation.4 | async-start | bytes 32768 | tf_op jit(solution)/shard_map/all_to_all | solution.py:134
  259.3 4.5 %copy-start.5 = (f32[1024,128]{1,0:T(8,128)S(1)}, f32[1024,128]{1,0:T(8,128)}, u32[]{:S(2)}) copy-start(f32[1024,128]{1,0:T(8,128)} %convolution_add_fusion.3) | copy-start | bytes 1572868
  263.8 5.2 %copy-start.7 = (f32[1024,128]{1,0:T(8,128)S(1)}, f32[1024,128]{1,0:T(8,128)}, u32[]{:S(2)}) copy-start(f32[1024,128]{1,0:T(8,128)} %convolution_add_fusion.2) | copy-start | bytes 1572868
  269.2 9.5 %copy-start.10 = (f32[128,4,256]{2,0,1:T(8,128)S(1)}, f32[128,4,256]{2,0,1:T(8,128)}, u32[]{:S(2)}) copy-start(f32[128,4,256]{2,0,1:T(8,128)} %copy.199) | copy-start | bytes 1572868
  271.1 14.9 %all-to-all-start.3 = ((f32[128,16,2]{0,2,1:T(2,128)}), f32[128,16,2]{0,2,1:T(2,128)S(1)}, u32[]{:S(2)}, u32[]{:S(2)}) async-start(f32[128,16,2]{0,2,1:T(2,128)} %copy.200), calls=%async_computation.3 | async-start | bytes 32768 | tf_op jit(solution)/shard_map/all_to_all | solution.py:131
  286.0 43.0 %all-to-all-start.2 = ((f32[128,16,256]{2,0,1:T(8,128)}), f32[128,16,256]{2,0,1:T(8,128)S(1)}, u32[]{:S(2)}, u32[]{:S(2)}) async-start(f32[128,16,256]{2,0,1:T(8,128)} %pad_maximum_fusion), calls=%async_computation.2 | async-start | bytes 4194304 | tf_op jit(solution)/shard_map/all_to_all | solution.py:137
  300.5 61.0 %copy-start.23 = (s32[64]{0:T(128)S(1)}, s32[64]{0:T(128)}, u32[]{:S(2)}) copy-start(s32[64]{0:T(128)} %copy-done.22) | copy-start | bytes 772
Sparse Core Ops, SparseCore 0:
  10.5 103.3 all-gather.2
  133.8 70.3 all-gather.4
where the time goes:
time: 370 us; the launch traced here: 369 us
  waiting for transfers between devices  199 us (54%)
  local copies, waits for them, and re-layouts  48.6 us (13%)
  blocking collectives  44.7 us (12%)
  matrix products  27.1 us (7%)
  starting transfers between devices  20.1 us (5%)
  other arithmetic  15.4 us (4%)
  between operations  14.6 us (4%)
    all_gather x1, waiting for transfers between devices, local(): lax.all_gather(w_proj, 'grp', axis=0, tiled=True)  104 us
    all_gather x1, waiting for transfers between devices, local(): lax.all_gather(received, 'tp', axis=2, tiled=True)  53 us
    all_to_all x1, blocking collectives, local(): lax.all_to_all(attended_slots, 'grp', split_axis=0, concat_axis=0, tiled=...  30.5 us
    all_to_all x1, waiting for transfers between devices, local(): lax.all_to_all(sums.reshape(slots, ranks, per_rank * head_dim), 'tp', spl...  28.5 us
    all_to_all x1, blocking collectives, local(): lax.all_to_all(packed, 'grp', split_axis=0, concat_axis=0, tiled=True)  14.2 us
    concatenate x8, local copies, waits for them, and re-layouts, local(): sums = jnp.concatenate(sums_list, axis=1)  9.27 us
    all_gather x1, local copies, waits for them, and re-layouts, local(): lax.all_gather(received, 'tp', axis=2, tiled=True)  8.71 us
    mul x2, local copies, waits for them, and re-layouts, local(): mixed = jnp.sum(parts_mixed * factor[..., None], axis=0)  8.69 us
  transfers between devices with their start and end apart: 6, of which 5 were waited for; matrix products, arithmetic and copies ran while one was open for 9% of the time, Pallas kernels for 0%

commit v1 on v0

v1 whole, which is shorter than its diff:
```python
import functools
import math

import jax
import jax.numpy as jnp
import numpy as np
from jax import lax
from jax.experimental import pallas as pl
from jax.experimental.pallas import tpu as pltpu
from jax.sharding import PartitionSpec as P

HD = 128
NEGATIVE = -1e30
THETA = 1000000.0
CAP = 4
F32 = jnp.float32
BF16 = jnp.bfloat16


def iota(shape, axis):
    return lax.broadcasted_iota(jnp.int32, shape, axis)


def nt(left, right):
    return lax.dot_general(left, right, (((1,), (1,)), ((), ())), preferred_element_type=F32)


def nn(left, right):
    return jnp.dot(left, right, preferred_element_type=F32)


def rotated(values, cosine, sine):
    return values * cosine + pltpu.roll(values, HD // 2, 1) * sine


def kernel(
    groups, ranks,
    hid_hbm, w_hbm, ck_hbm, cv_hbm, issue_ref, length_ref, prefix_ref, freq_ref,
    out_ref,
    hid, wbuf, kbuf, vbuf, acc, qs, qr, kvs, kvx, rs, rr,
    load_sem, w_send, w_x, w_ring, w_sib, c_send, c_recv, q_sem, kv_send, kv_recv, r_sem,
):
    g = lax.axis_index("grp")
    t = lax.axis_index("tp")
    x_hi = g // 16
    y = (g // 2) % 8
    core = g % 2
    block = ck_hbm.shape[1]
    rows = hid.shape[0]
    depth = w_hbm.shape[1]
    cols = w_hbm.shape[0]
    half = cols // 2

    def place(xx, yy, cc):
        return xx * 16 + lax.rem(yy + 8, 8) * 2 + cc

    right = place(x_hi, y + 1, core)
    left = place(x_hi, y - 1, core)
    partner = place(1 - x_hi, y, core)
    sibling = place(x_hi, y, 1 - core)

    load_hid = pltpu.make_async_copy(hid_hbm, hid, load_sem.at[0])
    load_hid.start()
    load_w = pltpu.make_async_copy(w_hbm, wbuf.at[g], load_sem.at[1])
    load_w.start()
    my_head = pl.multiple_of((t // 4) * HD, HD)
    my_rows = pl.ds(pl.multiple_of(t * block, block), block)
    load_k = pltpu.make_async_copy(ck_hbm.at[0, :, pl.ds(my_head, HD)], kbuf.at[my_rows], load_sem.at[2])
    load_k.start()
    load_v = pltpu.make_async_copy(cv_hbm.at[0, :, pl.ds(my_head, HD)], vbuf.at[my_rows], load_sem.at[3])
    load_v.start()

    barrier = pltpu.get_barrier_semaphore()

    def greet_grp(step, carry):
        pl.semaphore_signal(barrier, inc=1, device_id={"grp": lax.rem(g + step, groups)},
                            device_id_type=pl.DeviceIdType.MESH)
        return carry

    def greet_tp(step, carry):
        pl.semaphore_signal(barrier, inc=1, device_id={"tp": lax.rem(t + step, ranks)},
                            device_id_type=pl.DeviceIdType.MESH)
        return carry

    lax.fori_loop(1, groups, greet_grp, 0)
    lax.fori_loop(1, ranks, greet_tp, 0)
    pl.semaphore_wait(barrier, groups + ranks - 2)

    sends = []

    def push(source, index, part, arrived, target):
        copy = pltpu.make_async_remote_copy(
            src_ref=source, dst_ref=wbuf.at[index] if part is None else wbuf.at[index, part],
            send_sem=w_send.at[len(sends)], recv_sem=arrived,
            device_id={"grp": target}, device_id_type=pl.DeviceIdType.MESH)
        copy.start()
        sends.append(copy)

    def pull(index, part, arrived):
        where = wbuf.at[index] if part is None else wbuf.at[index, part]
        pltpu.make_async_remote_copy(
            src_ref=where, dst_ref=where, send_sem=w_send.at[0], recv_sem=arrived,
            device_id={"grp": sibling}, device_id_type=pl.DeviceIdType.MESH).wait_recv()

    def ring(line, way, hop):
        return w_ring.at[line * 8 + way * 4 + hop - 1]

    def sib(line, kind):
        return w_sib.at[line * 9 + kind]

    push(w_hbm, g, None, w_x.at[0], partner)
    push(w_hbm, g, None, ring(0, 0, 1), right)
    push(w_hbm, g, None, ring(0, 1, 1), left)
    push(w_hbm, g, None, sib(0, 0), sibling)

    def cache_copy(step, which):
        other = lax.rem(t + step, ranks)
        head = pl.ds(pl.multiple_of((other // 4) * HD, HD), HD)
        source, dest = ((ck_hbm, kbuf), (cv_hbm, vbuf))[which]
        return pltpu.make_async_remote_copy(
            src_ref=source.at[0, :, head], dst_ref=dest.at[my_rows],
            send_sem=c_send.at[which], recv_sem=c_recv.at[which],
            device_id={"tp": other}, device_id_type=pl.DeviceIdType.MESH)

    def send_cache(step, carry):
        cache_copy(step, 0).start()
        cache_copy(step, 1).start()
        return carry

    lax.fori_loop(1, ranks, send_cache, 0)

    lane = iota((1, 2 * rows), 1) & (rows - 1)
    down = iota((rows, 1), 0)
    issue_l = jnp.zeros((1, 2 * rows), jnp.int32)
    start_l = jnp.zeros((1, 2 * rows), jnp.int32)
    issue_d = jnp.zeros((rows, 1), jnp.int32)
    start_d = jnp.zeros((rows, 1), jnp.int32)
    begin = jnp.int32(0)
    for entry in range(issue_ref.shape[0]):
        end = begin + length_ref[entry]
        name = issue_ref[entry]
        in_l = (lane >= begin) & (lane < end)
        in_d = (down >= begin) & (down < end)
        issue_l = jnp.where(in_l, name, issue_l)
        start_l = jnp.where(in_l, begin, start_l)
        issue_d = jnp.where(in_d, name, issue_d)
        start_d = jnp.where(in_d, begin, start_d)
        begin = end
    pos_l = lane - start_l
    pos_d = down - start_d
    slot_l = issue_l * CAP + pos_l
    slot_d = issue_d * CAP + pos_d

    prefix = prefix_ref[0]
    sign = jnp.where(iota((1, HD), 1) < HD // 2, -1.0, 1.0).astype(F32)
    freq = freq_ref[0:1, :]
    angle_q = (prefix + (iota((8, 1), 0) & 3)).astype(F32) * freq
    cos_q = jnp.cos(angle_q)
    sin_q = jnp.sin(angle_q) * sign
    angle_o = pos_d.astype(F32) * freq
    cos_o = jnp.cos(angle_o)
    sin_o = jnp.sin(angle_o) * sign

    def mac(index):
        part = pl.ds(pl.multiple_of(index * depth, depth), depth)
        acc[...] += nt(hid[:, part], wbuf[index])

    acc[...] = jnp.zeros_like(acc)
    load_hid.wait()
    load_w.wait()
    mac(g)

    low, high = pl.ds(0, half), pl.ds(half, half)
    where_x = (x_hi, 1 - x_hi)

    def from_sibling(line, hop):
        if hop == 0:
            index = place(where_x[line], y, 1 - core)
            pull(index, None, sib(line, 0))
            mac(index)
        elif hop < 4:
            for way, yy in ((0, y - hop), (1, y + hop)):
                index = place(where_x[line], yy, 1 - core)
                pull(index, None, sib(line, 1 + way * 4 + hop - 1))
                mac(index)
        else:
            index = place(where_x[line], y + 4, 1 - core)
            pull(index, low, sib(line, 4))
            pull(index, high, sib(line, 8))
            mac(index)

    def from_ring(line, hop):
        if hop < 4:
            indices = []
            for way, yy, nxt, part in ((0, y - hop, right, low), (1, y + hop, left, high)):
                index = place(where_x[line], yy, core)
                pull(index, None, ring(line, way, hop))
                if hop < 3:
                    push(wbuf.at[index], index, None, ring(line, way, hop + 1), nxt)
                else:
                    push(wbuf.at[index, part], index, part, ring(line, way, 4), nxt)
                push(wbuf.at[index], index, None, sib(line, 1 + way * 4 + hop - 1), sibling)
                indices.append(index)
            for index in indices:
                mac(index)
        else:
            index = place(where_x[line], y + 4, core)
            for way, part in ((0, low), (1, high)):
                pull(index, part, ring(line, way, 4))
                push(wbuf.at[index, part], index, part, sib(line, 4 + way * 4), sibling)
            mac(index)

    def from_partner():
        pull(partner, None, w_x.at[0])
        push(wbuf.at[partner], partner, None, ring(1, 0, 1), right)
        push(wbuf.at[partner], partner, None, ring(1, 1, 1), left)
        push(wbuf.at[partner], partner, None, sib(1, 0), sibling)
        mac(partner)

    from_sibling(0, 0)
    from_ring(0, 1)
    from_partner()
    from_ring(0, 2)
    from_sibling(0, 1)
    from_sibling(1, 0)
    from_ring(1, 1)
    from_ring(0, 3)
    from_sibling(0, 2)
    from_ring(1, 2)
    from_sibling(1, 1)
    from_ring(0, 4)
    from_sibling(0, 3)
    from_ring(1, 3)
    from_sibling(1, 2)
    from_sibling(0, 4)
    from_ring(1, 4)
    from_sibling(1, 3)
    from_sibling(1, 4)

    proj = acc[...].astype(BF16)
    stacked = jnp.concatenate([proj[:, :HD], proj[:, HD:2 * HD]], axis=0)
    row = iota((8 * groups, 2 * rows), 0)
    pick = ((row >> 3) * CAP + (row & 3) == slot_l) & (
        ((row >> 2) & 1) == (iota((8 * groups, 2 * rows), 1) >= rows).astype(jnp.int32))
    qs[...] = nn(pick.astype(F32).astype(BF16), stacked)

    my_q = pl.ds(pl.multiple_of(g * 8, 8), 8)

    def q_copy(step):
        other = lax.rem(g + step, groups)
        return pltpu.make_async_remote_copy(
            src_ref=qs.at[pl.ds(pl.multiple_of(other * 8, 8), 8)], dst_ref=qr.at[my_q],
            send_sem=q_sem.at[0], recv_sem=q_sem.at[1],
            device_id={"grp": other}, device_id_type=pl.DeviceIdType.MESH)

    def send_q(step, carry):
        q_copy(step).start()
        return carry

    lax.fori_loop(1, groups, send_q, 0)
    qr[my_q, :] = qs[my_q, :]

    kvs[...] = jnp.concatenate([proj[:, 2 * HD:], jnp.zeros((rows, 2 * HD - (cols - 2 * HD) - HD), BF16)], axis=1)
    base = (t // 4) * 4
    kv_copies = []
    for step in (1, 2, 3):
        other = base + lax.rem(t + step, 4)
        copy = pltpu.make_async_remote_copy(
            src_ref=kvs, dst_ref=kvx.at[lax.rem(t, 4)],
            send_sem=kv_send.at[step], recv_sem=kv_recv.at[lax.rem(t, 4)],
            device_id={"tp": other}, device_id_type=pl.DeviceIdType.MESH)
        copy.start()
        kv_copies.append(copy)
    kvx[lax.rem(t, 4)] = kvs[...]

    load_k.wait()
    load_v.wait()
    rest = pl.ds(0, block * (ranks - 1))
    for which, dest in ((0, kbuf), (1, vbuf)):
        pltpu.make_async_remote_copy(
            src_ref=dest.at[rest], dst_ref=dest.at[rest], send_sem=c_send.at[which], recv_sem=c_recv.at[which],
            device_id={"grp": sibling}, device_id_type=pl.DeviceIdType.MESH).wait()
    rest_q = pl.ds(0, 8 * (groups - 1))
    pltpu.make_async_remote_copy(
        src_ref=qs.at[rest_q], dst_ref=qr.at[rest_q], send_sem=q_sem.at[0], recv_sem=q_sem.at[1],
        device_id={"grp": sibling}, device_id_type=pl.DeviceIdType.MESH).wait()

    scale = 1.0 / math.sqrt(HD)
    tall = 8 * groups
    full = (groups, 8, HD)
    query = rotated(qr[...], jnp.broadcast_to(cos_q[None], full).reshape(tall, HD),
                    jnp.broadcast_to(sin_q[None], full).reshape(tall, HD)).astype(BF16)
    score = nt(query, kbuf[...])
    early = iota((1, block * ranks), 1) < prefix
    score = jnp.where(early, score * scale, NEGATIVE)
    top = jnp.max(score, axis=1, keepdims=True)
    weight = jnp.exp(score - top)
    total = jnp.sum(weight, axis=1, keepdims=True)
    mixed = nn(weight.astype(BF16), vbuf[...]) / total
    level = jnp.broadcast_to(top + jnp.log(total), (tall, HD))
    hi = level.astype(BF16).astype(F32)
    mid = (level - hi).astype(BF16).astype(F32)
    lo = level - hi - mid
    across = iota((tall, HD), 1)
    stats = jnp.where(across < 32, hi, jnp.where(across < 64, mid, lo))
    rs[...] = jnp.concatenate([mixed.reshape(full), stats.reshape(full)], axis=1).astype(BF16)

    def r_copy(step):
        other = lax.rem(g + step, groups)
        return pltpu.make_async_remote_copy(
            src_ref=rs.at[other], dst_ref=rr.at[g],
            send_sem=r_sem.at[0], recv_sem=r_sem.at[1],
            device_id={"grp": other}, device_id_type=pl.DeviceIdType.MESH)

    def send_r(step, carry):
        r_copy(step).start()
        return carry

    lax.fori_loop(1, groups, send_r, 0)
    rr[g] = rs[g]

    for step in (1, 2, 3):
        source = lax.rem(t + step, 4)
        pltpu.make_async_remote_copy(
            src_ref=kvs, dst_ref=kvx.at[source], send_sem=kv_send.at[step], recv_sem=kv_recv.at[source],
            device_id={"grp": sibling}, device_id_type=pl.DeviceIdType.MESH).wait_recv()
    wide = jnp.concatenate([kvx[0], kvx[1], kvx[2], kvx[3]], axis=1)
    a = iota((4 * HD, 2 * HD), 0)
    b = iota((4 * HD, 2 * HD), 1)
    lane_a = a & (HD - 1)
    goal = (lane_a >> 5) * HD + (a >> 7) * 32 + (lane_a & 31)
    spread = ((goal == b) & (lane_a < 64)).astype(F32).astype(BF16)
    both = nn(wide, spread)
    keys = rotated(both[:, :HD], cos_o, sin_o).astype(BF16)
    values = both[:, HD:].astype(BF16)
    same = (issue_d == issue_l[:, :rows]) & (pos_l[:, :rows] <= pos_d)
    own = []
    for head in range(2):
        mine = rotated(proj[:, head * HD:(head + 1) * HD].astype(F32), cos_o, sin_o).astype(BF16)
        part = jnp.where(same, nt(mine, keys) * scale, NEGATIVE)
        peak = jnp.max(part, axis=1, keepdims=True)
        share = jnp.where(same, jnp.exp(part - peak), 0.0)
        own.append((peak, jnp.sum(share, axis=1, keepdims=True), nn(share.astype(BF16), values)))

    big = 16 * groups
    r = iota((rows, big), 1)
    hit = (r >> 4) * CAP + (r & 3) == slot_d
    field = (r >> 2) & 3
    picks = [(hit & (field == kind)).astype(F32).astype(BF16) for kind in range(4)]

    rest_r = pl.ds(0, groups - 1)
    pltpu.make_async_remote_copy(
        src_ref=rs.at[rest_r], dst_ref=rr.at[rest_r], send_sem=r_sem.at[0], recv_sem=r_sem.at[1],
        device_id={"grp": sibling}, device_id_type=pl.DeviceIdType.MESH).wait()
    back = rr[...].reshape(big, HD)
    for head in range(2):
        cached = nn(picks[head], back)
        told = nn(picks[2 + head], back)
        log_c = told[:, 0:1] + told[:, 32:33] + told[:, 64:65]
        peak, total_o, mixed_o = own[head]
        summit = jnp.maximum(peak, log_c)
        part_o = jnp.exp(peak - summit)
        part_c = jnp.exp(log_c - summit)
        value = (mixed_o * part_o + cached * part_c) / (total_o * part_o + part_c)
        out_ref[:, head * HD:(head + 1) * HD] = value.astype(BF16)

    for copy in kv_copies:
        copy.wait_send()
    for copy in sends:
        copy.wait_send()


def local(groups, ranks, hidden, w_proj, cache_keys, cache_values, cand_issue, cand_length, prefix_len):
    rows, model = hidden.shape
    depth, cols = w_proj.shape
    block = cache_keys.shape[1]
    spot = np.arange(HD) % (HD // 2)
    freq = np.broadcast_to((THETA ** (-2.0 * spot / HD)).astype(np.float32), (8, HD))
    any_space = pl.BlockSpec(memory_space=pl.ANY)
    smem = pl.BlockSpec(memory_space=pltpu.SMEM)
    vmem = pl.BlockSpec(memory_space=pltpu.VMEM)
    dma = pltpu.SemaphoreType.DMA
    return pl.pallas_call(
        functools.partial(kernel, groups, ranks),
        out_shape=jax.ShapeDtypeStruct((rows, 2 * HD), BF16),
        in_specs=[any_space] * 4 + [smem] * 3 + [vmem],
        out_specs=vmem,
        scratch_shapes=[
            pltpu.VMEM((rows, model), BF16),
            pltpu.VMEM((groups, cols, depth), BF16),
            pltpu.VMEM((block * ranks, HD), BF16),
            pltpu.VMEM((block * ranks, HD), BF16),
            pltpu.VMEM((rows, cols), F32),
            pltpu.VMEM((8 * groups, HD), F32),
            pltpu.VMEM((8 * groups, HD), F32),
            pltpu.VMEM((rows, HD), BF16),
            pltpu.VMEM((4, rows, HD), BF16),
            pltpu.VMEM((groups, 16, HD), BF16),
            pltpu.VMEM((groups, 16, HD), BF16),
            dma((4,)), dma((40,)), dma((1,)), dma((16,)), dma((18,)), dma((2,)), dma((2,)), dma((2,)),
            dma((4,)), dma((4,)), dma((2,)),
        ],
        compiler_params=pltpu.CompilerParams(
            collective_id=0, has_side_effects=True, vmem_limit_bytes=48 * 1024 * 1024),
        cost_estimate=pl.CostEstimate(flops=10**9, bytes_accessed=2 * 10**6, transcendentals=10**6),
    )(hidden, w_proj.T, cache_keys, cache_values, cand_issue, cand_length, prefix_len, jnp.asarray(freq))


def solution(mesh):
    placed = (
        P("grp", None),
        P("grp", "tp"),
        P("grp", "tp", None),
        P("grp", "tp", None),
        P("grp"),
        P("grp"),
        P("grp"),
    )
    return jax.shard_map(
        functools.partial(local, mesh.shape["grp"], mesh.shape["tp"]),
        mesh=mesh, in_specs=placed, out_specs=P("grp", "tp"), check_vma=False)
```

time: 370 us -> 78.5 us (0.21)
  waiting for transfers between devices: 199 us -> 0 us
  Pallas kernels: 0 us -> 71.7 us
  blocking collectives: 44.7 us -> 0 us
  local copies, waits for them, and re-layouts: 48.6 us -> 5.88 us
  matrix products: 27.1 us -> 0 us
  starting transfers between devices: 20.1 us -> 0 us
  other arithmetic: 15.4 us -> 0 us
  between operations: 14.6 us -> 0.68 us
    all_gather x2 -> x0, waiting for transfers between devices: 157 us -> none  [the longest x1 104 us: local(): lax.all_gather(w_proj, 'grp', axis=0, tiled=True)]
    pallas_call x0 -> x1, Pallas kernels: none -> 71.7 us  [local(): pl.pallas_call(functools.partial(kernel, groups, ranks), out_shape=jax.Sh...]
    all_to_all x2 -> x0, blocking collectives: 44.7 us -> none  [the longest x1 30.5 us: local(): lax.all_to_all(attended_slots, 'grp', split_axis=0, concat_axis=0, tiled=...]
    all_to_all x4 -> x0, waiting for transfers between devices: 40.6 us -> none  [the longest x1 28.5 us: local(): lax.all_to_all(sums.reshape(slots, ranks, per_rank * head_dim), 'tp', spl...]
    dot_general x18 -> x0, matrix products: 27.1 us -> none  [the longest x4 7.75 us: local(): jnp.dot(w_p.astype(jnp.bfloat16), cached_v, preferred_element_type=jnp.fl...]
    all_to_all x4 -> x0, starting transfers between devices: 20.1 us -> none  [the longest x1 7.56 us: local(): lax.all_to_all(maxima.reshape(slots, ranks, per_rank), 'tp', split_axis=1...]
    concatenate x10 -> x0, local copies, waits for them, and re-layouts: 11.3 us -> none  [the longest x8 9.27 us: local(): sums = jnp.concatenate(sums_list, axis=1)]
    all_gather x1 -> x0, local copies, waits for them, and re-layouts: 8.71 us -> none  [local(): lax.all_gather(received, 'tp', axis=2, tiled=True)]
  transfers between devices with their start and end apart: 6 -> 0, of which waited for: 5 -> 0; matrix products, arithmetic and copies ran while one was open for 9% -> 0% of each run, Pallas kernels for 0% -> 0%
where the time goes in v1:
time: 78.5 us; the launch traced here: 78.3 us
  Pallas kernels  71.7 us (91%)
  local copies, waits for them, and re-layouts  5.88 us (7%)
    pallas_call x1, Pallas kernels, local(): pl.pallas_call(functools.partial(kernel, groups, ranks), out_shape=jax.Sh...  71.7 us
    unnamed x15, local copies, waits for them, and re-layouts  5.88 us

profile of v1, /device:TPU:1, one launch (start us, length us, event | category | flops | bytes accessed | tf_op | source)
XLA Modules:
  0.0 78.3 jit_solution(13840002985101791809)
XLA Ops:
  0.7 0.0 copy-start.6
  0.7 0.6 copy-done.6
  1.3 0.0 copy-start.4
  1.3 0.0 copy-start.5
  1.3 0.6 copy-done.4
  2.0 0.0 copy-done.5
  2.0 0.0 copy-start
  2.0 1.2 %copy-done = bf16[64,8192]{1,0:T(8,128)(2,1)S(1)} copy-done((bf16[64,8192]{1,0:T(8,128)(2,1)S(1)}, bf16[64,8192]{1,0:T(8,128)(2,1)}, u32[]{:S(2)}) %copy-start) | copy-done | bytes 1048600
  3.2 0.0 copy-start.1
  3.2 0.9 %copy-done.1 = bf16[256,320]{0,1:T(8,128)(2,1)S(1)} copy-done((bf16[256,320]{0,1:T(8,128)(2,1)S(1)}, bf16[256,320]{0,1:T(8,128)(2,1)}, u32[]{:S(2)}) %copy-start.1) | copy-done | bytes 163864
  4.1 0.0 copy-start.2
  4.1 0.9 %copy-done.2 = bf16[1,128,512]{2,1,0:T(8,128)(2,1)S(1)} copy-done((bf16[1,128,512]{2,1,0:T(8,128)(2,1)S(1)}, bf16[1,128,512]{2,1,0:T(8,128)(2,1)}, u32[]{:S(2)}) %copy-start.2) | copy-done | bytes 131096
  5.0 0.0 copy-start.3
  5.0 0.9 %copy-done.3 = bf16[1,128,512]{2,1,0:T(8,128)(2,1)S(1)} copy-done((bf16[1,128,512]{2,1,0:T(8,128)(2,1)S(1)}, bf16[1,128,512]{2,1,0:T(8,128)(2,1)}, u32[]{:S(2)}) %copy-start.3) | copy-done | bytes 131096
  5.9 71.7 %shard_map.82 = bf16[64,256]{1,0:T(8,128)(2,1)S(1)} custom-call(bf16[64,8192]{1,0:T(8,128)(2,1)S(1)} %copy-done, bf16[320,256]{1,0:T(8,128)(2,1)S(1)} %bitcast.1, bf16[1,128,512]{2,1,0:T(8,128)(2,1)S(1)} %copy-done.2, bf16[1,128,512]{2,1,0:T(8,128)(2,1)S(1)} %copy-done.3, s32[32]{0:T(128)S(1)} %copy-done.4, s32[32]{0:T(128)S(1)} %copy-done.5, ...), custom_call_target="tpu_custom_call" | custom-call | flops 1000000000 | bytes 2000000 | tf_op jit(solution)/shard_map/pallas_call | solution.py:383
  77.6 0.6 copy.11
  (1 shorter events, 0.0 us)
Async XLA Ops:
  0.7 0.7 copy-start.6
  1.3 0.7 copy-start.4
  1.3 0.7 copy-start.5
  2.0 1.2 %copy-start = (bf16[64,8192]{1,0:T(8,128)(2,1)S(1)}, bf16[64,8192]{1,0:T(8,128)(2,1)}, u32[]{:S(2)}) copy-start(bf16[64,8192]{1,0:T(8,128)(2,1)} %hid_hbm.1) | copy-start | bytes 3145732
  3.2 0.9 %copy-start.1 = (bf16[256,320]{0,1:T(8,128)(2,1)S(1)}, bf16[256,320]{0,1:T(8,128)(2,1)}, u32[]{:S(2)}) copy-start(bf16[256,320]{0,1:T(8,128)(2,1)} %param.9) | copy-start | bytes 491524
  4.1 0.9 %copy-start.2 = (bf16[1,128,512]{2,1,0:T(8,128)(2,1)S(1)}, bf16[1,128,512]{2,1,0:T(8,128)(2,1)}, u32[]{:S(2)}) copy-start(bf16[1,128,512]{2,1,0:T(8,128)(2,1)} %ck_hbm.1) | copy-start | bytes 393220
  5.0 0.9 %copy-start.3 = (bf16[1,128,512]{2,1,0:T(8,128)(2,1)S(1)}, bf16[1,128,512]{2,1,0:T(8,128)(2,1)}, u32[]{:S(2)}) copy-start(bf16[1,128,512]{2,1,0:T(8,128)(2,1)} %cv_hbm.1) | copy-start | bytes 393220

commit v2 on v1

--- a/solution.py
+++ b/solution.py
@@ -37,8 +37,8 @@
     groups, ranks,
     hid_hbm, w_hbm, ck_hbm, cv_hbm, issue_ref, length_ref, prefix_ref, freq_ref,
     out_ref,
-    hid, wbuf, kbuf, vbuf, acc, qs, qr, kvs, kvx, rs, rr,
-    load_sem, w_send, w_x, w_ring, w_sib, c_send, c_recv, q_sem, kv_send, kv_recv, r_sem,
+    hid, wbuf, kbuf, vbuf, acc, px, qs, qr, kvs, kvx, rs, rr,
+    load_sem, w_send, w_ring, w_sib, h_send, h_recv, p_sem, c_send, c_recv, q_sem, kv_send, kv_recv, r_sem,
 ):
     g = lax.axis_index("grp")
     t = lax.axis_index("tp")
@@ -46,7 +46,8 @@
     y = (g // 2) % 8
     core = g % 2
     block = ck_hbm.shape[1]
-    rows = hid.shape[0]
+    rows = hid_hbm.shape[0]
+    span = hid_hbm.shape[1] // 2
     depth = w_hbm.shape[1]
     cols = w_hbm.shape[0]
     half = cols // 2
@@ -59,9 +60,10 @@
     partner = place(1 - x_hi, y, core)
     sibling = place(x_hi, y, 1 - core)
 
-    load_hid = pltpu.make_async_copy(hid_hbm, hid, load_sem.at[0])
+    my_span = pl.ds(pl.multiple_of(x_hi * span, span), span)
+    load_hid = pltpu.make_async_copy(hid_hbm.at[:, my_span], hid.at[0:rows], load_sem.at[0])
     load_hid.start()
-    load_w = pltpu.make_async_copy(w_hbm, wbuf.at[g], load_sem.at[1])
+    load_w = pltpu.make_async_copy(w_hbm, wbuf.at[lax.rem(g, 16)], load_sem.at[1])
     load_w.start()
     my_head = pl.multiple_of((t // 4) * HD, HD)
     my_rows = pl.ds(pl.multiple_of(t * block, block), block)
@@ -84,7 +86,9 @@
 
     lax.fori_loop(1, groups, greet_grp, 0)
     lax.fori_loop(1, ranks, greet_tp, 0)
-    pl.semaphore_wait(barrier, groups + ranks - 2)
+    pl.semaphore_signal(barrier, inc=1, device_id={"grp": partner, "tp": lax.rem(t + 8, ranks)},
+                        device_id_type=pl.DeviceIdType.MESH)
+    pl.semaphore_wait(barrier, groups + ranks - 1)
 
     sends = []
 
@@ -102,16 +106,28 @@
             src_ref=where, dst_ref=where, send_sem=w_send.at[0], recv_sem=arrived,
             device_id={"grp": sibling}, device_id_type=pl.DeviceIdType.MESH).wait_recv()
 
-    def ring(line, way, hop):
-        return w_ring.at[line * 8 + way * 4 + hop - 1]
-
-    def sib(line, kind):
-        return w_sib.at[line * 9 + kind]
-
-    push(w_hbm, g, None, w_x.at[0], partner)
-    push(w_hbm, g, None, ring(0, 0, 1), right)
-    push(w_hbm, g, None, ring(0, 1, 1), left)
-    push(w_hbm, g, None, sib(0, 0), sibling)
+    def ring(way, hop):
+        return w_ring.at[way * 4 + hop - 1]
+
+    def line(yy, cc):
+        return lax.rem(yy + 8, 8) * 2 + cc
+
+    mine = line(y, core)
+    push(w_hbm, mine, None, ring(0, 1), right)
+    push(w_hbm, mine, None, ring(1, 1), left)
+    push(w_hbm, mine, None, w_sib.at[0], sibling)
+
+    def hid_copy(order, yy):
+        far = pl.ds(pl.multiple_of((1 - x_hi) * span + lax.rem(yy + 8, 8) * 2 * depth, 2 * depth), 2 * depth)
+        near = pl.ds(pl.multiple_of(lax.rem(yy + 8, 8) * 2 * depth, 2 * depth), 2 * depth)
+        return pltpu.make_async_remote_copy(
+            src_ref=hid_hbm.at[:, far], dst_ref=hid.at[rows:2 * rows, near],
+            send_sem=h_send.at[order], recv_sem=h_recv.at[order],
+            device_id={"grp": partner, "tp": lax.rem(t + 8, ranks)}, device_id_type=pl.DeviceIdType.MESH)
+
+    hid_copies = [hid_copy(order, y + step) for order, step in enumerate((0, -1, 1, -2, 2, -3, 3, 4))]
+    for copy in hid_copies:
+        copy.start()
 
     def cache_copy(step, which):
         other = lax.rem(t + step, ranks)
@@ -168,76 +184,67 @@
     acc[...] = jnp.zeros_like(acc)
     load_hid.wait()
     load_w.wait()
-    mac(g)
+    hid_copies[0].wait_recv()
+    mac(mine)
 
     low, high = pl.ds(0, half), pl.ds(half, half)
-    where_x = (x_hi, 1 - x_hi)
-
-    def from_sibling(line, hop):
+
+    def from_sibling(hop):
         if hop == 0:
-            index = place(where_x[line], y, 1 - core)
-            pull(index, None, sib(line, 0))
+            index = line(y, 1 - core)
+            pull(index, None, w_sib.at[0])
             mac(index)
         elif hop < 4:
             for way, yy in ((0, y - hop), (1, y + hop)):
-                index = place(where_x[line], yy, 1 - core)
-                pull(index, None, sib(line, 1 + way * 4 + hop - 1))
+                index = line(yy, 1 - core)
+                pull(index, None, w_sib.at[1 + way * 4 + hop - 1])
                 mac(index)
         else:
-            index = place(where_x[line], y + 4, 1 - core)
-            pull(index, low, sib(line, 4))
-            pull(index, high, sib(line, 8))
+            index = line(y + 4, 1 - core)
+            pull(index, low, w_sib.at[4])
+            pull(index, high, w_sib.at[8])
             mac(index)
 
-    def from_ring(line, hop):
+    def from_ring(hop):
         if hop < 4:
             indices = []
             for way, yy, nxt, part in ((0, y - hop, right, low), (1, y + hop, left, high)):
-                index = place(where_x[line], yy, core)
-                pull(index, None, ring(line, way, hop))
+                index = line(yy, core)
+                pull(index, None, ring(way, hop))
                 if hop < 3:
-                    push(wbuf.at[index], index, None, ring(line, way, hop + 1), nxt)
+                    push(wbuf.at[index], index, None, ring(way, hop + 1), nxt)
                 else:
-                    push(wbuf.at[index, part], index, part, ring(line, way, 4), nxt)
-                push(wbuf.at[index], index, None, sib(line, 1 + way * 4 + hop - 1), sibling)
+                    push(wbuf.at[index, part], index, part, ring(way, 4), nxt)
+                push(wbuf.at[index], index, None, w_sib.at[1 + way * 4 + hop - 1], sibling)
                 indices.append(index)
-            for index in indices:
+            for way, index in enumerate(indices):
+                hid_copies[hop * 2 - 1 + way].wait_recv()
                 mac(index)
         else:
-            index = place(where_x[line], y + 4, core)
+            index = line(y + 4, core)
             for way, part in ((0, low), (1, high)):
-                pull(index, part, ring(line, way, 4))
-                push(wbuf.at[index, part], index, part, sib(line, 4 + way * 4), sibling)
+                pull(index, part, ring(way, 4))
+                push(wbuf.at[index, part], index, part, w_sib.at[4 + way * 4], sibling)
+            hid_copies[7].wait_recv()
             mac(index)
 
-    def from_partner():
-        pull(partner, None, w_x.at[0])
-        push(wbuf.at[partner], partner, None, ring(1, 0, 1), right)
-        push(wbuf.at[partner], partner, None, ring(1, 1, 1), left)
-        push(wbuf.at[partner], partner, None, sib(1, 0), sibling)
-        mac(partner)
-
-    from_sibling(0, 0)
-    from_ring(0, 1)
-    from_partner()
-    from_ring(0, 2)
-    from_sibling(0, 1)
-    from_sibling(1, 0)
-    from_ring(1, 1)
-    from_ring(0, 3)
-    from_sibling(0, 2)
-    from_ring(1, 2)
-    from_sibling(1, 1)
-    from_ring(0, 4)
-    from_sibling(0, 3)
-    from_ring(1, 3)
-    from_sibling(1, 2)
-    from_sibling(0, 4)
-    from_ring(1, 4)
-    from_sibling(1, 3)
-    from_sibling(1, 4)
-
-    proj = acc[...].astype(BF16)
+    from_sibling(0)
+    from_ring(1)
+    from_sibling(1)
+    from_ring(2)
+    from_sibling(2)
+    from_ring(3)
+    from_sibling(3)
+    from_ring(4)
+    from_sibling(4)
+
+    swap = pltpu.make_async_remote_copy(
+        src_ref=acc.at[rows:2 * rows], dst_ref=px, send_sem=p_sem.at[0], recv_sem=p_sem.at[1],
+        device_id={"grp": partner}, device_id_type=pl.DeviceIdType.MESH)
+    swap.start()
+    swap.wait_recv()
+
+    proj = (acc[0:rows, :] + px[...]).astype(BF16)
     stacked = jnp.concatenate([proj[:, :HD], proj[:, HD:2 * HD]], axis=0)
     row = iota((8 * groups, 2 * rows), 0)
     pick = ((row >> 3) * CAP + (row & 3) == slot_l) & (
@@ -366,7 +373,7 @@
 
     for copy in kv_copies:
         copy.wait_send()
-    for copy in sends:
+    for copy in sends + hid_copies + [swap]:
         copy.wait_send()
 
 
@@ -386,10 +393,11 @@
         in_specs=[any_space] * 4 + [smem] * 3 + [vmem],
         out_specs=vmem,
         scratch_shapes=[
-            pltpu.VMEM((rows, model), BF16),
-            pltpu.VMEM((groups, cols, depth), BF16),
+            pltpu.VMEM((2 * rows, model // 2), BF16),
+            pltpu.VMEM((groups // 2, cols, depth), BF16),
             pltpu.VMEM((block * ranks, HD), BF16),
             pltpu.VMEM((block * ranks, HD), BF16),
+            pltpu.VMEM((2 * rows, cols), F32),
             pltpu.VMEM((rows, cols), F32),
             pltpu.VMEM((8 * groups, HD), F32),
             pltpu.VMEM((8 * groups, HD), F32),
@@ -397,11 +405,11 @@
             pltpu.VMEM((4, rows, HD), BF16),
             pltpu.VMEM((groups, 16, HD), BF16),
             pltpu.VMEM((groups, 16, HD), BF16),
-            dma((4,)), dma((40,)), dma((1,)), dma((16,)), dma((18,)), dma((2,)), dma((2,)), dma((2,)),
+            dma((4,)), dma((20,)), dma((8,)), dma((9,)), dma((8,)), dma((8,)), dma((2,)), dma((2,)), dma((2,)), dma((2,)),
             dma((4,)), dma((4,)), dma((2,)),
         ],
         compiler_params=pltpu.CompilerParams(
-            collective_id=0, has_side_effects=True, vmem_limit_bytes=48 * 1024 * 1024),
+            collective_id=0, has_side_effects=True, vmem_limit_bytes=60 * 1024 * 1024),
         cost_estimate=pl.CostEstimate(flops=10**9, bytes_accessed=2 * 10**6, transcendentals=10**6),
     )(hidden, w_proj.T, cache_keys, cache_values, cand_issue, cand_length, prefix_len, jnp.asarray(freq))
 

time: 78.5 us -> 61.9 us (0.79)
  Pallas kernels: 71.7 us -> 58.4 us
  local copies, waits for them, and re-layouts: 5.88 us -> 2.62 us
    pallas_call x1, Pallas kernels: 71.7 us -> 58.4 us  [local(): pl.pallas_call(functools.partial(kernel, groups, ranks), out_shape=jax.Sh...]
    unnamed x15 -> x3, local copies, waits for them, and re-layouts: 5.88 us -> 2.03 us
where the time goes in v2:
time: 61.9 us; the launch traced here: 61.7 us
  Pallas kernels  58.4 us (94%)
  local copies, waits for them, and re-layouts  2.62 us (4%)
  between operations  0.67 us (1%)
    pallas_call x1, Pallas kernels, local(): pl.pallas_call(functools.partial(kernel, groups, ranks), out_shape=jax.Sh...  58.4 us
    unnamed x3, local copies, waits for them, and re-layouts  2.03 us

profile of v2, /device:TPU:1, one launch (start us, length us, event | category | flops | bytes accessed | tf_op | source)
XLA Modules:
  0.0 61.7 jit_solution(13477831579937742458)
XLA Ops:
  0.7 0.0 copy-start
  0.7 0.6 %copy-done = f32[128]{0:T(128)S(1)} copy-done((f32[128]{0:T(128)S(1)}, f32[128]{0:T(128)}, u32[]{:S(2)}) %copy-start) | copy-done | bytes 536
  1.3 0.6 jit_solution_.3.freq_ref
  1.9 58.4 %shard_map.82 = bf16[64,256]{1,0:T(8,128)(2,1)} custom-call(bf16[64,8192]{1,0:T(8,128)(2,1)} %hid_hbm.1, bf16[320,256]{1,0:T(8,128)(2,1)} %bitcast.1, bf16[1,128,512]{2,1,0:T(8,128)(2,1)} %ck_hbm.1, bf16[1,128,512]{2,1,0:T(8,128)(2,1)} %cv_hbm.1, s32[32]{0:T(128)} %issue_ref.1, s32[32]{0:T(128)} %length_ref.1, s32[1]{0:T(128)S(6)} %copy.10.prefix_ref, ...), custom_call_target="tpu_custom_call" | custom-call | flops 1000000000 | bytes 2000000 | tf_op jit(solution)/shard_map/pallas_call | solution.py:390
  60.3 1.4 %copy.11 = bf16[64,256]{1,0:T(8,128)(2,1)} copy(bf16[64,256]{1,0:T(8,128)(2,1)} %shard_map.82) | data formatting | bytes 65536
Async XLA Ops:
  0.7 0.7 %copy-start = (f32[128]{0:T(128)S(1)}, f32[128]{0:T(128)}, u32[]{:S(2)}) copy-start(f32[128]{0:T(128)} %constant.2.clone) | copy-start | bytes 1540
